TPU v7x, 512 devices: a whole 4x4x16 slice. The times are simulated.
512 devices in a mesh: row: 32 (over x, y, core), col: 16 (over z).
Axes of the slice: x: 4, y: 4, z: 16, core: 2. Of those that a mesh axis runs over, the one named last changes fastest.
Arguments:
- amplitudes: float32 [4096, 2, 256], P(('row', 'col')), may hold values from -18 to 18
- integrals: float32 [2, 256, 102400], P(None, 'row', 'col'), may hold values from -0.25 to 0.25
- occ_pairs: int32 [4096, 2], P('row'), may hold values from 0 to 199
- eps_occ: float32 [200], replicated, may hold values from -2 to -0.5
- eps_vir: float32 [800], replicated, may hold values from 0.2 to 3
- vir_offset: int32 [1], replicated, may hold values from 0 to 672
Outputs:
- update: float32 [4096, 102400], P('row', 'col')
All inputs are finite; a program needn't handle non-finite values.
Results may differ from a plain program's by a relative error of at most 0.00007.
Values sent between devices are 32-bit elements; how exact they have to be, the bound alone decides.
A program may use at most 64 MiB of HBM per device.

v0:
```python
import jax
import jax.numpy as jnp
from jax import lax
from jax.sharding import PartitionSpec as P


def shards(amplitudes, integrals, occ_pairs, eps_occ, eps_vir, vir_offset):
    amp_full = lax.all_gather(amplitudes, "col", axis=0, tiled=True)
    pair_rows = amp_full.shape[0]
    tile_width = integrals.shape[2]
    empty = jnp.zeros((pair_rows, tile_width), jnp.float32)
    ladder = empty
    for position in range(integrals.shape[0]):
        int_block = lax.all_gather(integrals[position], "row", axis=0, tiled=True)
        ladder = ladder + jnp.dot(
            amp_full[:, position, :],
            int_block,
            preferred_element_type=jnp.float32,
            precision=lax.Precision.HIGHEST,
        )
    pair_energy = eps_occ[occ_pairs[:, 0]] + eps_occ[occ_pairs[:, 1]]
    a_count = tile_width // eps_vir.shape[0]
    a_start = vir_offset[0] + lax.axis_index("col") * a_count
    block_energy = lax.dynamic_slice(eps_vir, (a_start,), (a_count,))
    vir_energy = (block_energy[:, None] + eps_vir[None, :]).reshape(-1)
    return ladder / (pair_energy[:, None] - vir_energy[None, :])


def solution(mesh):
    return jax.shard_map(
        shards,
        mesh=mesh,
        in_specs=(
            P(("row", "col"), None, None),
            P(None, "row", "col"),
            P("row", None),
            P(),
            P(),
            P(),
        ),
        out_specs=P("row", "col"),
        check_vma=False,
    )
```

profile of v0, /device:TPU:1, one launch (start us, length us, event | category | flops | bytes accessed | tf_op | source)
XLA Modules:
  0.0 163.8 jit_solution(384103486761567337)
XLA Ops:
  6.5 0.0 copy-start
  6.5 0.0 all-gather.5.cloned.1.call-start
  6.5 1.8 %fusion.6 = (f32[1,8,6400]{2,1,0:T(8,128)}, f32[1,8,6400]{2,1,0:T(8,128)}) fusion(f32[2,8,6400]{2,1,0:T(8,128)} %param.7), kind=kLoop, calls=%fused_computation.16 | loop fusion | bytes 819200 | tf_op jit(solution)/shard_map/slice | solution.py:14
  8.4 0.0 all-gather.5.cloned.1.call-update
  8.4 0.0 all-gather.7.cloned.1.call-start
  8.5 0.7 all-gather.7.cloned.1.call-update
  9.2 0.7 copy.7
  10.5 0.8 dynamic_slice.3
  11.3 0.8 broadcast_add_fusion
  12.1 0.7 add.53
  12.7 0.8 fusion.5
  13.5 0.0 copy-done
  13.5 1.3 gather_fusion
  14.8 1.3 gather_fusion.1
  16.1 30.6 %all_gather.9 = f32[128,2,256]{2,0,1:T(8,128)S(1)} all-gather(f32[8,2,256]{2,0,1:T(8,128)S(1)} %copy.7), channel_id=1, replica_groups=mesh['row'=32,'col'=16] {'col'}, dimensions={0}, use_global_device_ids=true | all-gather | bytes 278528 | tf_op jit(solution)/shard_map/all_gather | solution.py:8
  46.7 34.4 %all-gather.5.cloned.1.call-done = f32[1,256,6400]{2,1,0:T(8,128)} async-done(((f32[1,8,6400]{2,1,0:T(8,128)}), f32[1,256,6400]{2,1,0:T(8,128)}) %all-gather.5.cloned.1.call-update) | async-done | bytes 6553616 | tf_op jit(solution)/shard_map/all_gather | solution.py:14
  81.1 5.7 %fusion.2 = f32[128,6400]{1,0:T(8,128)S(1)} fusion(f32[1,256,6400]{2,1,0:T(8,128)} %all-gather.5.cloned.1.call-done, f32[128,2,256]{2,0,1:T(8,128)S(1)} %all_gather.9), kind=kOutput, calls=%fused_computation.5 | convolution fusion | flops 2516582400 | bytes 9961472 | tf_op jit(solution)/shard_map/dot_general | solution.py:15
  86.8 61.3 %all-gather.7.cloned.1.call-done = f32[1,256,6400]{2,1,0:T(8,128)} async-done(((f32[1,8,6400]{2,1,0:T(8,128)}), f32[1,256,6400]{2,1,0:T(8,128)}) %all-gather.7.cloned.1.call-update) | async-done | bytes 6553616 | tf_op jit(solution)/shard_map/all_gather | solution.py:14
  148.1 8.8 %fusion = f32[128,6400]{1,0:T(8,128)} fusion(f32[128,6400]{1,0:T(8,128)S(1)} %fusion.2, f32[1,256,6400]{2,1,0:T(8,128)} %all-gather.7.cloned.1.call-done, f32[6400]{0:T(1024)} %add.53, f32[128]{0:T(128)S(1)} %add.47, f32[128,2,256]{2,0,1:T(8,128)S(1)} %all_gather.9), kind=kOutput, calls=%fused_computation.3 | convolution fusion | flops 2519040000 | bytes 13264384 | tf_op jit(solution)/shard_map/dot_general | solution.py:15
  (2 shorter events, 0.0 us)
Async XLA Ops:
  6.5 7.0 %copy-start = (f32[200]{0:T(256)S(1)}, f32[200]{0:T(256)}, u32[]{:S(2)}) copy-start(f32[200]{0:T(256)} %param.9) | copy-start | bytes 2404
  6.5 74.6 %all-gather.5.cloned.1.call-start = ((), (), s32[]{:S(2)}) async-start(), calls=%async_computation | async-start | bytes 6758400 | tf_op jit(solution)/shard_map/all_gather | solution.py:14
  8.4 139.7 %all-gather.7.cloned.1.call-start = ((), (), s32[]{:S(2)}) async-start(), calls=%async_computation.1 | async-start | bytes 6758400 | tf_op jit(solution)/shard_map/all_gather | solution.py:14
Sparse Core Ops, SparseCore 0:
  10.5 70.5 all-gather.4
  84.2 63.8 all-gather.6
where the time goes:
time: 164 us
  waiting for transfers between devices  96.4 us (59%)
  blocking collectives  30.6 us (19%)
  matrix products  14.5 us (9%)
  between operations  14.1 us (9%)
  local copies, waits for them, and re-layouts  6.55 us (4%)
    all_gather x2, waiting for transfers between devices, shards(): int_block = lax.all_gather(integrals[position], 'row', axis=0, tiled=True)  95.7 us
    all_gather x1, blocking collectives, shards(): amp_full = lax.all_gather(amplitudes, 'col', axis=0, tiled=True)  30.6 us
    dot_general x2, matrix products, shards(): jnp.dot(amp_full[:, position, :], int_block, preferred_element_type=jnp.f...  14.5 us
  transfers between devices with their start and end apart: 2, of which 2 were waited for; matrix products, arithmetic and copies ran while one was open for 7% of the time, Pallas kernels for 0%

commit v1 on v0

v1 whole, which is shorter than its diff:
```python
import functools

import jax
import jax.numpy as jnp
from jax import lax
from jax.experimental import pallas as pl
from jax.experimental.pallas import tpu as pltpu
from jax.sharding import PartitionSpec as P

MESH = pl.DeviceIdType.MESH
SIDE = 4
DEPTH = 16
WIDTH = 640
AHEAD = 3


def gather_kernel(
    amp_ref, int_ref, occ_ref, eocc_ref, evir_ref, off_ref, out_ref,
    rows, amps, both, pair, vir,
    send, recv, zsend, zrecv, own,
):
    row, z = lax.axis_index("row"), lax.axis_index("col")
    x, y, core = row // 8, (row // 2) % SIDE, row % 2
    way = 1 - 2 * core
    width = WIDTH
    parts = int_ref.shape[2] // width

    def at(xx, yy, cc):
        return {"row": (xx * SIDE + yy) * 2 + cc, "col": z}

    def along(panel, first, step):
        to = (lambda v: (v + step + SIDE) % SIDE)
        if (panel == 0) == first:
            return at(to(x), y, core)
        return at(x, to(y), core)

    sibling = at(x, y, 1 - core)
    peers = [along(0, True, 1), along(0, True, -1), along(0, False, 1), along(0, False, -1), sibling]
    peers += [{"row": row, "col": (z + j) % DEPTH} for j in range(1, DEPTH)]
    barrier = pltpu.get_barrier_semaphore()
    for peer in peers:
        pl.semaphore_signal(barrier, inc=1, device_id=peer, device_id_type=MESH)
    pl.semaphore_wait(barrier, len(peers))

    def cols(k):
        return pl.ds(k * width, width)

    def copy(kind, panel, k, src, dst, to):
        return pltpu.make_async_remote_copy(
            src_ref=src, dst_ref=dst, send_sem=send.at[kind, panel, k], recv_sem=recv.at[kind, panel, k],
            device_id=to, device_id_type=MESH,
        )

    def one(panel, k, back):
        if panel == 0:
            return rows.at[0, (x - back + SIDE) % SIDE, y, core, :, cols(k)]
        return rows.at[1, x, (y - back + SIDE) % SIDE, core, :, cols(k)]

    def line(panel, k, back):
        if panel == 0:
            return rows.at[0, :, (y - back + SIDE) % SIDE, core, :, cols(k)]
        return rows.at[1, (x - back + SIDE) % SIDE, :, core, :, cols(k)]

    def ahead(p, k):
        return copy(0, p, k, int_ref.at[p, :, cols(k)], one(p, k, 0), along(p, True, way))

    def behind(p, k):
        return copy(1, p, k, int_ref.at[p, :, cols(k)], one(p, k, 0), along(p, True, -way))

    def onward(p, k):
        src = one(p, k, way)
        return copy(2, p, k, src, src, along(p, True, way))

    def line_ahead(p, k):
        src = line(p, k, 0)
        return copy(3, p, k, src, src, along(p, False, way))

    def line_behind(p, k):
        src = line(p, k, 0)
        return copy(4, p, k, src, src, along(p, False, -way))

    def line_onward(p, k):
        src = line(p, k, way)
        return copy(5, p, k, src, src, along(p, False, way))

    def across(p, k):
        src = rows.at[p, :, :, core, :, cols(k)]
        return copy(6, p, k, src, src, sibling)

    both_panels = (0, 1)
    own_copy = pltpu.make_async_copy(int_ref, rows.at[:, x, y, core], own.at[0])
    own_copy.start()
    amp_copy = pltpu.make_async_copy(amp_ref, amps.at[z], own.at[1])
    amp_copy.start()

    def start_own(k):
        for p in both_panels:
            ahead(p, k).start()
            behind(p, k).start()

    start_own(0)

    def amp_send(j):
        return pltpu.make_async_remote_copy(
            src_ref=amp_ref, dst_ref=amps.at[z], send_sem=zsend.at[j], recv_sem=zrecv.at[j],
            device_id={"row": row, "col": (z + j) % DEPTH}, device_id_type=MESH,
        )

    for k in range(1, AHEAD):
        start_own(k)
    for j in range(1, DEPTH):
        amp_send(j).start()

    lanes = lax.broadcasted_iota(jnp.int32, (occ_ref.shape[0], eocc_ref.shape[1]), 1)
    energy = eocc_ref[...]
    occ_sum = jnp.sum(jnp.where(lanes == occ_ref[:, 0:1], energy, 0.0), axis=1, keepdims=True)
    occ_sum = occ_sum + jnp.sum(jnp.where(lanes == occ_ref[:, 1:2], energy, 0.0), axis=1, keepdims=True)
    pair[...] = jnp.broadcast_to(occ_sum, pair.shape)
    virtual = evir_ref[...]
    spots = lax.broadcasted_iota(jnp.int32, virtual.shape, 1)
    count = int_ref.shape[2] // virtual.shape[1]
    first = off_ref[0] + z * count
    vir[...] = jnp.concatenate(
        [jnp.sum(jnp.where(spots == first + a, virtual, 0.0), axis=1, keepdims=True) + virtual for a in range(count)],
        axis=1,
    )

    def split_amps():
        amp_copy.wait()
        for j in range(1, DEPTH):
            amp_send(j).wait()
        high_low = amps[...].reshape(both.shape[0] // 2, both.shape[1])
        high = high_low.astype(jnp.bfloat16)
        both[: high.shape[0], :] = high
        both[high.shape[0] :, :] = (high_low - high.astype(jnp.float32)).astype(jnp.bfloat16)

    def compute(k):
        n = out_ref.shape[0]
        block = rows[:, :, :, :, :, cols(k)].reshape(both.shape[1], width)
        high = block.astype(jnp.bfloat16)
        low = (block - high.astype(jnp.float32)).astype(jnp.bfloat16)
        head = jnp.dot(both[...], high, preferred_element_type=jnp.float32)
        tail = jnp.dot(both[:n, :], low, preferred_element_type=jnp.float32)
        ladder = head[:n] + (head[n:] + tail)
        energy = pair[:, 0:1] - vir[:, cols(k)]
        out_ref[:, cols(k)] = ladder / energy

    for t in range(parts + 5):
        if AHEAD <= t + AHEAD < parts:
            start_own(t + AHEAD)
        if t < parts:
            for p in both_panels:
                ahead(p, t).wait_recv()
                onward(p, t).start()
        k = t - 1
        if 0 <= k < parts:
            if k == 0:
                own_copy.wait()
            for p in both_panels:
                behind(p, k).wait_recv()
                onward(p, k).wait_recv()
                line_ahead(p, k).start()
                line_behind(p, k).start()
        k = t - 3
        if 0 <= k < parts:
            for p in both_panels:
                line_ahead(p, k).wait_recv()
                line_onward(p, k).start()
        k = t - 4
        if 0 <= k < parts:
            for p in both_panels:
                line_behind(p, k).wait_recv()
                line_onward(p, k).wait_recv()
                across(p, k).start()
        k = t - 5
        if 0 <= k < parts:
            if k == 0:
                split_amps()
            for p in both_panels:
                across(p, k).wait_recv()
            compute(k)

    for k in range(parts):
        for p in both_panels:
            for made in (ahead, behind, onward, line_ahead, line_behind, line_onward, across):
                made(p, k).wait_send()


def store_kernel(src_ref, dst_ref, sems):
    count = sems.shape[0]
    height = src_ref.shape[0] // count
    copies = [
        pltpu.make_async_copy(src_ref.at[pl.ds(i * height, height)], dst_ref.at[pl.ds(i * height, height)], sems.at[i])
        for i in range(count)
    ]
    for one in copies:
        one.start()
    for one in copies:
        one.wait()


def shards(amplitudes, integrals, occ_pairs, eps_occ, eps_vir, vir_offset):
    panels, depth, ab = integrals.shape
    mine, _, panel = amplitudes.shape
    pairs = occ_pairs.shape[0]
    cd = panels * panel
    parts = ab // WIDTH
    vmem = pl.BlockSpec(memory_space=pltpu.VMEM)
    update = pl.pallas_call(
        gather_kernel,
        out_shape=pltpu.VMEM((pairs, ab), jnp.float32),
        in_specs=[vmem, pl.BlockSpec(memory_space=pl.ANY), vmem, vmem, vmem, pl.BlockSpec(memory_space=pltpu.SMEM)],
        out_specs=vmem,
        scratch_shapes=[
            pltpu.VMEM((panels, SIDE, SIDE, 2, depth, ab), jnp.float32),
            pltpu.VMEM((DEPTH, mine, cd), jnp.float32),
            pltpu.VMEM((2 * pairs, cd), jnp.bfloat16),
            pltpu.VMEM((pairs, 128), jnp.float32),
            pltpu.VMEM((1, ab), jnp.float32),
            pltpu.SemaphoreType.DMA((7, 2, parts)),
            pltpu.SemaphoreType.DMA((7, 2, parts)),
            pltpu.SemaphoreType.DMA((DEPTH,)),
            pltpu.SemaphoreType.DMA((DEPTH,)),
            pltpu.SemaphoreType.DMA((2,)),
        ],
        compiler_params=pltpu.CompilerParams(
            collective_id=0, has_side_effects=True, vmem_limit_bytes=40 * 1024 * 1024
        ),
        cost_estimate=pl.CostEstimate(
            flops=2 * pairs * cd * ab * 3, bytes_accessed=4 * (pairs * ab + panels * depth * ab), transcendentals=0
        ),
        name="gather_and_contract",
    )(
        amplitudes.reshape(mine, cd),
        integrals,
        occ_pairs,
        eps_occ.reshape(1, -1),
        eps_vir.reshape(1, -1),
        vir_offset,
    )
    return pl.pallas_call(
        store_kernel,
        out_shape=jax.ShapeDtypeStruct((pairs, ab), jnp.float32),
        in_specs=[vmem],
        out_specs=pl.BlockSpec(memory_space=pl.ANY),
        scratch_shapes=[pltpu.SemaphoreType.DMA((8,))],
        cost_estimate=pl.CostEstimate(flops=0, bytes_accessed=4 * pairs * ab, transcendentals=0),
        name="store",
    )(pltpu.with_memory_space_constraint(update, pltpu.VMEM))


def solution(mesh):
    return jax.shard_map(
        shards,
        mesh=mesh,
        in_specs=(
            P(("row", "col"), None, None),
            P(None, "row", "col"),
            P("row", None),
            P(),
            P(),
            P(),
        ),
        out_specs=P("row", "col"),
        check_vma=False,
    )
```

time: 164 us -> 71.7 us (0.44)
  waiting for transfers between devices: 96.4 us -> 0 us
  Pallas kernels: 0 us -> 66.9 us
  blocking collectives: 30.6 us -> 0 us
  matrix products: 14.5 us -> 0 us
  between operations: 14.1 us -> 0.67 us
  local copies, waits for them, and re-layouts: 6.55 us -> 3.87 us
    all_gather x2 -> x0, waiting for transfers between devices: 95.7 us -> none  [shards(): int_block = lax.all_gather(integrals[position], 'row', axis=0, tiled=True)]
    pallas_call x0 -> x2, Pallas kernels: none -> 66.9 us  [the longest x1 65.1 us: shards(): pl.pallas_call(gather_kernel, out_shape=pltpu.VMEM((pairs, ab), jnp.float...]
    all_gather x1 -> x0, blocking collectives: 30.6 us -> none  [shards(): amp_full = lax.all_gather(amplitudes, 'col', axis=0, tiled=True)]
    dot_general x2 -> x0, matrix products: 14.5 us -> none  [shards(): jnp.dot(amp_full[:, position, :], int_block, preferred_element_type=jnp.f...]
    gather x2 -> x0, local copies, waits for them, and re-layouts: 2.54 us -> none  [shards(): pair_energy = eps_occ[occ_pairs[:, 0]] + eps_occ[occ_pairs[:, 1]]]
    unnamed x3 -> x6, local copies, waits for them, and re-layouts: 0.73 us -> 3.18 us
    slice x1 -> x0, local copies, waits for them, and re-layouts: 1.84 us -> none  [shards(): int_block = lax.all_gather(integrals[position], 'row', axis=0, tiled=True)]
  transfers between devices with their start and end apart: 2 -> 0, of which waited for: 2 -> 0; matrix products, arithmetic and copies ran while one was open for 7% -> 0% of each run, Pallas kernels for 0% -> 0%
where the time goes in v1:
time: 71.7 us; the launch traced here: 71.4 us
  Pallas kernels  66.9 us (93%)
  local copies, waits for them, and re-layouts  3.87 us (5%)
    pallas_call x1, Pallas kernels, shards(): pl.pallas_call(gather_kernel, out_shape=pltpu.VMEM((pairs, ab), jnp.float...  65.1 us
    unnamed x6, local copies, waits for them, and re-layouts  3.18 us
    pallas_call x1, Pallas kernels, shards(): pl.pallas_call(store_kernel, out_shape=jax.ShapeDtypeStruct((pairs, ab),...  1.77 us

profile of v1, /device:TPU:1, one launch (start us, length us, event | category | flops | bytes accessed | tf_op | source)
XLA Modules:
  0.0 71.4 jit_solution(6151540268568653779)
XLA Ops:
  0.7 0.7 reshape.11.evir_ref
  1.3 0.7 %copy.8 = f32[1,8,2,256]{3,1,2,0:T(8,128)S(1)} copy(f32[1,8,2,256]{3,2,1,0:T(2,128)} %bitcast.5) | data formatting | bytes 32768
  2.1 0.8 %copy.7.occ_ref = s32[128,2]{1,0:T(8,128)S(1)} copy(s32[128,2]{0,1:T(2,128)} %param.8) | data formatting | bytes 2048 | tf_op args[2]
  2.8 0.0 copy-start
  2.9 1.0 %copy-done = f32[2,8,6400]{2,1,0:T(8,128)S(1)} copy-done((f32[2,8,6400]{2,1,0:T(8,128)S(1)}, f32[2,8,6400]{2,1,0:T(8,128)}, u32[]{:S(2)}) %copy-start) | copy-done | bytes 409624
  3.8 0.0 copy-start.1
  3.9 0.7 copy-done.1
  4.5 65.1 %gather_and_contract.1.src_ref = f32[128,6400]{1,0:T(8,128)S(1)} custom-call(f32[8,512]{1,0:T(8,128)S(1)} %bitcast.3, f32[2,8,6400]{2,1,0:T(8,128)S(1)} %copy-done, s32[128,2]{1,0:T(8,128)S(1)} %copy.7.occ_ref, f32[1,200]{1,0:T(1,128)S(1)} %bitcast.4, f32[1,800]{1,0:T(1,128)S(1)} %reshape.11.evir_ref, s32[1]{0:T(128)S(6)} %copy.9.off_ref), custom_call_target="tpu_custom_call" | custom-call | flops 2516582400 | bytes 3686400 | tf_op jit(solution)/shard_map/gather_and_contract/pallas_call | solution.py:209
  69.6 1.8 %store.1 = f32[128,6400]{1,0:T(8,128)} custom-call(f32[128,6400]{1,0:T(8,128)S(1)} %gather_and_contract.1.src_ref), custom_call_target="tpu_custom_call" | custom-call | bytes 3276800 | tf_op jit(solution)/shard_map/store/pallas_call | solution.py:241
Async XLA Ops:
  2.8 1.0 %copy-start = (f32[2,8,6400]{2,1,0:T(8,128)S(1)}, f32[2,8,6400]{2,1,0:T(8,128)}, u32[]{:S(2)}) copy-start(f32[2,8,6400]{2,1,0:T(8,128)} %int_ref.1) | copy-start | bytes 1228804
  3.8 0.7 copy-start.1

commit v2 on v0

v2 whole, which is shorter than its diff:
```python
import functools

import jax
import jax.numpy as jnp
from jax import lax
from jax.experimental import pallas as pl
from jax.experimental.pallas import tpu as pltpu
from jax.sharding import PartitionSpec as P

MESH = pl.DeviceIdType.MESH
SIDE = 4
DEPTH = 16
PIECES = (640, 2560)
PARTS = (640, 768, 768, 640, 384)


def gather_kernel(
    amp_hbm, int_hbm, occ_hbm, eocc_hbm, evir_hbm, off_ref, out_ref,
    rows, slabs, amps, both, pair, vir, stage,
    amp_ref, occ_ref, eocc_ref, evir_ref,
    local, send, near, far, ring, side,
):
    row, z = lax.axis_index("row"), lax.axis_index("col")
    x, y, core = row // 8, (row // 2) % SIDE, row % 2
    way = 1 - 2 * core
    half = int_hbm.shape[2] // 2
    mine = pl.multiple_of(core * half, 128)
    pairs = out_ref.shape[0]
    panels = (0, 1)

    def shift(v, step, size=SIDE):
        return (v + step + size) % size

    def at(xx, yy, cc):
        return {"row": (xx * SIDE + yy) * 2 + cc, "col": z}

    def along(panel, phase, step, cc):
        if panel == phase:
            return at(shift(x, step), y, cc)
        return at(x, shift(y, step), cc)

    sibling = at(x, y, 1 - core)

    def fetch(i, src, dst):
        return pltpu.make_async_copy(src, dst, local.at[i])

    fetches = [
        fetch(0, int_hbm.at[:, :, pl.ds(mine, half)], rows.at[:, x, y, core]),
        fetch(1, amp_hbm, amp_ref),
        fetch(2, occ_hbm, occ_ref),
        fetch(3, eocc_hbm, eocc_ref),
        fetch(4, evir_hbm, evir_ref),
    ]
    for one in fetches:
        one.start()

    peers = [along(0, phase, step, cc) for phase in (0, 1) for step in (1, -1) for cc in (0, 1)]
    peers += [sibling] + [{"row": row, "col": shift(z, step, DEPTH)} for step in (1, -1)]
    barrier = pltpu.get_barrier_semaphore()
    for peer in peers:
        pl.semaphore_signal(barrier, inc=1, device_id=peer, device_id_type=MESH)
    pl.semaphore_wait(barrier, len(peers))

    def remote(src, dst, sent, got, to):
        return pltpu.make_async_remote_copy(
            src_ref=src, dst_ref=dst, send_sem=sent, recv_sem=got, device_id=to, device_id_type=MESH
        )

    starts = [sum(PIECES[:a]) for a in range(len(PIECES))]

    def chip(p, a, back):
        cols = pl.ds(starts[a], PIECES[a])
        if p == 0:
            return rows.at[0, shift(x, -back), y, :, :, cols]
        return rows.at[1, x, shift(y, -back), :, :, cols]

    def first_direct(p, a, step, cc):
        src = int_hbm.at[p, :, pl.ds(cc * half + starts[a], PIECES[a])]
        dst = rows.at[p, x, y, core, :, pl.ds(starts[a], PIECES[a])]
        return remote(src, dst, send.at[0], near.at[(1 - step) // 2, p, a], along(p, 0, step, cc))

    def first(p, a, step):
        return remote(chip(p, a, 0), chip(p, a, 0), send.at[0], near.at[(1 - step) // 2, p, a], along(p, 0, step, core))

    def first_arrived(p, a, index):
        remote(chip(p, a, 0), chip(p, a, 0), send.at[0], near.at[index, p, a], sibling).wait_recv()

    def first_onward(p, a):
        return remote(chip(p, a, way), chip(p, a, way), send.at[0], near.at[2, p, a], along(p, 0, way, core))

    begins = [sum(PARTS[:k]) for k in range(len(PARTS))]

    def line(p, k, back):
        cols = pl.ds(begins[k], PARTS[k])
        if p == 0:
            return rows.at[0, :, shift(y, -back), :, :, cols]
        return rows.at[1, shift(x, -back), :, :, :, cols]

    def second(p, k, kind):
        back, step = ((0, way), (0, -way), (way, way))[kind]
        return remote(line(p, k, back), line(p, k, back), send.at[1], far.at[kind, p, k], along(p, 1, step, core))

    steps = DEPTH // 2
    base = core * steps

    def ring_copy(s):
        src = slabs.at[0] if s == 1 else slabs.at[base + s - 1]
        return remote(src, slabs.at[base + s], send.at[2], ring.at[s - 1], {"row": row, "col": shift(z, way, DEPTH)})

    halves = remote(
        int_hbm.at[:, :, pl.ds(pl.multiple_of((1 - core) * half, 128), half)],
        rows.at[:, x, y, core], send.at[3], side.at[0], sibling,
    )
    own_slab = remote(slabs.at[0, core], slabs.at[0, core], send.at[4], side.at[1], sibling)
    pair_copy = remote(pair.at[core], pair.at[core], send.at[5], side.at[2], sibling)
    share = remote(slabs.at[pl.ds(base + 1, steps)], slabs.at[pl.ds(base + 1, steps)], send.at[6], side.at[3], sibling)

    def result(k):
        cols = pl.ds(begins[k], PARTS[k])
        there = out_ref.at[:, pl.ds(pl.multiple_of(mine + begins[k], 128), PARTS[k])]
        return remote(stage.at[:, cols], there, send.at[7], side.at[4], sibling)

    halves.start()
    for p in panels:
        for step in (1, -1):
            for cc in (0, 1):
                first_direct(p, 0, step, cc).start()

    fetches[1].wait()
    width = amp_ref.shape[2]
    for p in panels:
        slabs[0, core, :, p * width : (p + 1) * width] = amp_ref[:, p, :]
    own_slab.start()
    fetches[0].wait()
    halves.wait_recv()
    for a in range(1, len(PIECES)):
        for p in panels:
            for step in (1, -1):
                first(p, a, step).start()
    for p in panels:
        first_arrived(p, 0, core)
        first_onward(p, 0).start()
    own_slab.wait_recv()
    ring_copy(1).start()

    for one in fetches[2:]:
        one.wait()
    occ_count = eocc_ref.shape[0]
    levels = jnp.broadcast_to(eocc_ref[...].reshape(1, occ_count), (pairs, occ_count)).T
    spots = lax.broadcasted_iota(jnp.int32, levels.shape, 0)
    energy = [jnp.sum(jnp.where(spots == occ_ref[i : i + 1, :], levels, 0.0), axis=0, keepdims=True) for i in (0, 1)]
    pair[core] = jnp.broadcast_to(energy[0] + energy[1], (pairs, pairs)).T
    pair_copy.start()
    virtual = evir_ref[...].reshape(1, evir_ref.shape[0])
    spots = lax.broadcasted_iota(jnp.int32, virtual.shape, 1)
    count = half // virtual.shape[1]
    lead = off_ref[0] + (2 * z + core) * count
    vir[...] = jnp.concatenate(
        [jnp.sum(jnp.where(spots == lead + a, virtual, 0.0), axis=1, keepdims=True) + virtual for a in range(count)],
        axis=1,
    )

    def ring_step(s):
        if s > steps:
            return
        ring_copy(s).wait_recv()
        if s < steps:
            ring_copy(s + 1).start()
        else:
            share.start()

    def split_amps():
        share.wait_recv()
        pair_copy.wait_recv()
        for j in range(DEPTH):
            back = -j if j <= steps else j - steps
            amps[shift(z, back, DEPTH)] = slabs[j]
        for i, c in enumerate((core, 1 - core)):
            full = amps[:, c].reshape(pairs, amps.shape[3])
            high = full.astype(jnp.bfloat16)
            both[i * pairs : (i + 1) * pairs, :] = high
            both[(2 + i) * pairs : (3 + i) * pairs, :] = (full - high.astype(jnp.float32)).astype(jnp.bfloat16)

    def compute(k):
        cols = pl.ds(begins[k], PARTS[k])
        block = rows[:, :, :, :, :, cols].reshape(both.shape[1], PARTS[k])
        high = block.astype(jnp.bfloat16)
        low = (block - high.astype(jnp.float32)).astype(jnp.bfloat16)
        head = jnp.dot(both[...], high, preferred_element_type=jnp.float32)
        tail = jnp.dot(both[: 2 * pairs, :], low, preferred_element_type=jnp.float32)
        ladder = head[: 2 * pairs] + (head[2 * pairs :] + tail)
        stage[:, cols] = ladder[pairs:] / (pair[1 - core][:, 0:1] - vir[:, cols])
        result(k).start()
        there = pl.ds(pl.multiple_of(mine + begins[k], 128), PARTS[k])
        out_ref[:, there] = ladder[:pairs] / (pair[core][:, 0:1] - vir[:, cols])

    def start_second(k):
        for p in panels:
            second(p, k, 0).start()
            second(p, k, 1).start()

    def onward_second(k):
        for p in panels:
            second(p, k, 0).wait_recv()
            second(p, k, 2).start()

    def finish(k):
        for p in panels:
            second(p, k, 1).wait_recv()
            second(p, k, 2).wait_recv()
        compute(k)

    for p in panels:
        first_arrived(p, 0, 1 - core)
        first_arrived(p, 0, 2)
    start_second(0)
    for a in range(1, len(PIECES)):
        for p in panels:
            first_arrived(p, a, core)
            first_onward(p, a).start()
    ring_step(1)
    for a in range(1, len(PIECES)):
        for p in panels:
            first_arrived(p, a, 1 - core)
            first_arrived(p, a, 2)
    count = len(PARTS)
    done = 2
    for k in range(1, count + 1):
        if k < count:
            start_second(k)
        if k == 1:
            ring_step(done)
            done += 1
        onward_second(k - 1)
        for _ in range(2):
            ring_step(done)
            done += 1
        if k == count - 1:
            while done <= steps:
                ring_step(done)
                done += 1
            split_amps()
            for j in range(count - 2):
                finish(j)
    finish(count - 2)
    finish(count - 1)

    remote(rows.at[0, 0:3, 0:2], rows.at[0, 0:3, 0:2], send.at[0], side.at[0], sibling).wait_send()
    remote(rows.at[:, :, 0:3], rows.at[:, :, 0:3], send.at[1], side.at[0], sibling).wait_send()
    remote(slabs.at[pl.ds(0, steps)], slabs.at[pl.ds(0, steps)], send.at[2], side.at[0], sibling).wait_send()
    for one in (halves, own_slab, pair_copy, share):
        one.wait_send()
    all_results = remote(stage, out_ref.at[:, pl.ds(mine, half)], send.at[7], side.at[4], sibling)
    all_results.wait_send()
    all_results.wait_recv()


def store_kernel(src_ref, dst_ref, sems):
    count = sems.shape[0]
    height = src_ref.shape[0] // count
    copies = [
        pltpu.make_async_copy(src_ref.at[pl.ds(i * height, height)], dst_ref.at[pl.ds(i * height, height)], sems.at[i])
        for i in range(count)
    ]
    for one in copies:
        one.start()
    for one in copies:
        one.wait()


def gather_and_contract(amplitudes, integrals, occ_pairs, eps_occ, eps_vir, vir_offset, cid=0, name="gather_and_contract"):
    panels, depth, ab = integrals.shape
    mine, _, panel = amplitudes.shape
    pairs = occ_pairs.shape[0]
    cd = panels * panel
    half = ab // 2
    hbm = pl.BlockSpec(memory_space=pltpu.HBM)
    arrays = (amplitudes, integrals, occ_pairs.T, eps_occ, eps_vir)
    return pl.pallas_call(
        gather_kernel,
        out_shape=pltpu.VMEM((pairs, ab), jnp.float32),
        in_specs=[hbm] * 5 + [pl.BlockSpec(memory_space=pltpu.SMEM)],
        out_specs=pl.BlockSpec(memory_space=pltpu.VMEM),
        scratch_shapes=[
            pltpu.VMEM((panels, SIDE, SIDE, 2, depth, half), jnp.float32),
            pltpu.VMEM((DEPTH + 1, 2, mine, cd), jnp.float32),
            pltpu.VMEM((DEPTH, 2, mine, cd), jnp.float32),
            pltpu.VMEM((4 * pairs, cd), jnp.bfloat16),
            pltpu.VMEM((2, pairs, pairs), jnp.float32),
            pltpu.VMEM((1, half), jnp.float32),
            pltpu.VMEM((pairs, half), jnp.float32),
            pltpu.VMEM(amplitudes.shape, jnp.float32),
            pltpu.VMEM((2, pairs), jnp.int32),
            pltpu.VMEM(eps_occ.shape, jnp.float32),
            pltpu.VMEM(eps_vir.shape, jnp.float32),
            pltpu.SemaphoreType.DMA((5,)),
            pltpu.SemaphoreType.DMA((8,)),
            pltpu.SemaphoreType.DMA((3, 2, len(PIECES))),
            pltpu.SemaphoreType.DMA((3, 2, len(PARTS))),
            pltpu.SemaphoreType.DMA((DEPTH // 2,)),
            pltpu.SemaphoreType.DMA((5,)),
        ],
        compiler_params=pltpu.CompilerParams(
            collective_id=cid, has_side_effects=True, vmem_limit_bytes=40 * 1024 * 1024
        ),
        cost_estimate=pl.CostEstimate(
            flops=2 * pairs * cd * ab * 3, bytes_accessed=4 * (pairs * ab + panels * depth * ab), transcendentals=0
        ),
        name=name,
    )(*(pltpu.with_memory_space_constraint(a, pltpu.HBM) for a in arrays), vir_offset)


def shards(amplitudes, integrals, occ_pairs, eps_occ, eps_vir, vir_offset):
    update = gather_and_contract(amplitudes, integrals, occ_pairs, eps_occ, eps_vir, vir_offset)
    return pl.pallas_call(
        store_kernel,
        out_shape=jax.ShapeDtypeStruct(update.shape, jnp.float32),
        in_specs=[pl.BlockSpec(memory_space=pltpu.VMEM)],
        out_specs=pl.BlockSpec(memory_space=pl.ANY),
        scratch_shapes=[pltpu.SemaphoreType.DMA((8,))],
        cost_estimate=pl.CostEstimate(flops=0, bytes_accessed=4 * update.size, transcendentals=0),
        name="store",
    )(pltpu.with_memory_space_constraint(update, pltpu.VMEM))


def solution(mesh):
    return jax.shard_map(
        shards,
        mesh=mesh,
        in_specs=(
            P(("row", "col"), None, None),
            P(None, "row", "col"),
            P("row", None),
            P(),
            P(),
            P(),
        ),
        out_specs=P("row", "col"),
        check_vma=False,
    )
```

time: 164 us -> 61.1 us (0.37)
  waiting for transfers between devices: 96.4 us -> 0 us
  Pallas kernels: 0 us -> 60.4 us
  blocking collectives: 30.6 us -> 0 us
  matrix products: 14.5 us -> 0 us
  between operations: 14.1 us -> 0.66 us
  local copies, waits for them, and re-layouts: 6.55 us -> 0 us
    all_gather x2 -> x0, waiting for transfers between devices: 95.7 us -> none  [shards(): int_block = lax.all_gather(integrals[position], 'row', axis=0, tiled=True)]
    pallas_call x0 -> x2, Pallas kernels: none -> 60.4 us  [the longest x1 58.6 us: gather_and_contract(): pl.pallas_call(gather_kernel, out_shape=pltpu.VMEM((pairs, ab), jnp.float...]
    all_gather x1 -> x0, blocking collectives: 30.6 us -> none  [shards(): amp_full = lax.all_gather(amplitudes, 'col', axis=0, tiled=True)]
    dot_general x2 -> x0, matrix products: 14.5 us -> none  [shards(): jnp.dot(amp_full[:, position, :], int_block, preferred_element_type=jnp.f...]
    gather x2 -> x0, local copies, waits for them, and re-layouts: 2.54 us -> none  [shards(): pair_energy = eps_occ[occ_pairs[:, 0]] + eps_occ[occ_pairs[:, 1]]]
    slice x1 -> x0, local copies, waits for them, and re-layouts: 1.84 us -> none  [shards(): int_block = lax.all_gather(integrals[position], 'row', axis=0, tiled=True)]
  transfers between devices with their start and end apart: 2 -> 0, of which waited for: 2 -> 0; matrix products, arithmetic and copies ran while one was open for 7% -> 0% of each run, Pallas kernels for 0% -> 0%
where the time goes in v2:
time: 61.1 us; the launch traced here: 61 us
  Pallas kernels  60.4 us (99%)
  between operations  0.66 us (1%)
    pallas_call x1, Pallas kernels, gather_and_contract(): pl.pallas_call(gather_kernel, out_shape=pltpu.VMEM((pairs, ab), jnp.float...  58.6 us
    pallas_call x1, Pallas kernels, shards(): pl.pallas_call(store_kernel, out_shape=jax.ShapeDtypeStruct(update.shape,...  1.77 us

profile of v2, /device:TPU:1, one launch (start us, length us, event | category | flops | bytes accessed | tf_op | source)
XLA Modules:
  0.0 61.0 jit_solution(1245160067805657197)
XLA Ops:
  0.7 58.6 %gather_and_contract.1.src_ref = f32[128,6400]{1,0:T(8,128)S(1)} custom-call(f32[8,2,256]{2,1,0:T(2,128)} %amp_hbm.1, f32[2,8,6400]{2,1,0:T(8,128)} %int_hbm.1, s32[2,128]{1,0:T(2,128)} %bitcast.1, f32[200]{0:T(256)} %eocc_hbm.1, f32[800]{0:T(1024)} %evir_hbm.1, s32[1]{0:T(128)S(6)} %copy.7.off_ref), custom_call_target="tpu_custom_call" | custom-call | flops 2516582400 | bytes 3686400 | tf_op jit(solution)/shard_map/gather_and_contract/pallas_call | solution.py:279
  59.2 1.8 %store.1 = f32[128,6400]{1,0:T(8,128)} custom-call(f32[128,6400]{1,0:T(8,128)S(1)} %gather_and_contract.1.src_ref), custom_call_target="tpu_custom_call" | custom-call | bytes 3276800 | tf_op jit(solution)/shard_map/store/pallas_call | solution.py:315

commit v3 on v0

v3 whole, which is shorter than its diff:
```python
import functools

import jax
import jax.numpy as jnp
from jax import lax
from jax.experimental import pallas as pl
from jax.experimental.pallas import tpu as pltpu
from jax.sharding import PartitionSpec as P

MESH = pl.DeviceIdType.MESH
SIDE = 4
DEPTH = 16
REACH = 3
PIECES = (640, 2560)
PARTS = (640, 768, 768, 640, 384)


def gather_kernel(
    amp_hbm, int_hbm, occ_hbm, eocc_hbm, evir_hbm, off_ref, out_ref,
    rows, slabs, amps, both, pair, vir, stage,
    amp_ref, occ_ref, eocc_ref, evir_ref,
    local, send, near, onto, far, over, line_send, line_got, side,
):
    row, z = lax.axis_index("row"), lax.axis_index("col")
    x, y, core = row // 8, (row // 2) % SIDE, row % 2
    way = 1 - 2 * core
    half = int_hbm.shape[2] // 2
    mine = pl.multiple_of(core * half, 128)
    pairs = out_ref.shape[0]
    panels = (0, 1)

    def turn(v):
        return (v + SIDE) % SIDE

    def beside(axis, step, cc):
        if axis == 0:
            return {"row": (turn(x + step) * SIDE + y) * 2 + cc, "col": z}
        return {"row": (x * SIDE + turn(y + step)) * 2 + cc, "col": z}

    sibling = {"row": row + way, "col": z}

    def there(d):
        return jnp.logical_and(z + d >= 0, z + d < DEPTH)

    def fetch(i, src, dst):
        return pltpu.make_async_copy(src, dst, local.at[i])

    fetches = [
        fetch(0, int_hbm.at[:, :, pl.ds(mine, half)], rows.at[:, 0, 0, core]),
        fetch(1, amp_hbm, amp_ref),
        fetch(2, occ_hbm, occ_ref),
        fetch(3, eocc_hbm, eocc_ref),
        fetch(4, evir_hbm, evir_ref),
    ]
    for one in fetches:
        one.start()

    barrier = pltpu.get_barrier_semaphore()

    def greet(to):
        pl.semaphore_signal(barrier, inc=1, device_id=to, device_id_type=MESH)

    greeted = 9
    greet(sibling)
    for axis in (0, 1):
        for step in (1, -1):
            for cc in (0, 1):
                greet(beside(axis, step, cc))
    for d in range(1, REACH + 1):
        for dd in (d, -d):
            pl.when(there(dd))(functools.partial(greet, {"row": row, "col": z + dd}))
            greeted = greeted + there(dd).astype(jnp.int32)
    pl.semaphore_wait(barrier, greeted)

    def remote(src, dst, sent, got, to):
        return pltpu.make_async_remote_copy(
            src_ref=src, dst_ref=dst, send_sem=sent, recv_sem=got, device_id=to, device_id_type=MESH
        )

    starts = [sum(PIECES[:a]) for a in range(len(PIECES))]
    begins = [sum(PARTS[:k]) for k in range(len(PARTS))]

    def place(p, along_first, along_second, cols):
        if p == 0:
            return rows.at[0, along_first, along_second, :, :, cols]
        return rows.at[1, along_second, along_first, :, :, cols]

    def own_direct(axis, step, cc):
        src = int_hbm.at[:, :, pl.ds(pl.multiple_of(cc * half, 128), PIECES[0])]
        back = (-step) % SIDE
        spot = (slice(None), back, 0) if axis == 0 else (slice(None), 0, back)
        dst = rows.at[(*spot, core, slice(None), pl.ds(0, PIECES[0]))]
        return remote(src, dst, send.at[0], near.at[0, axis, 0, (1 - step) // 2], beside(axis, step, cc))

    def own_direct_arrived(axis, index):
        block = rows.at[:, 0, 0, :, :, pl.ds(0, PIECES[0])]
        remote(block, block, send.at[0], near.at[0, axis, 0, index], sibling).wait_recv()

    def own(a, p, phase, step):
        cols = pl.ds(starts[a], PIECES[a])
        back = (-step) % SIDE
        dst = place(p, back, 0, cols) if phase == 0 else place(p, 0, back, cols)
        axis = phase if p == 0 else 1 - phase
        return remote(place(p, 0, 0, cols), dst, send.at[0], near.at[a, p, phase, (1 - step) // 2], beside(axis, step, core))

    def own_arrived(a, p, phase, index):
        block = place(p, 0, 0, pl.ds(starts[a], PIECES[a]))
        remote(block, block, send.at[0], near.at[a, p, phase, index], sibling).wait_recv()

    def onward(a, p):
        cols = pl.ds(starts[a], PIECES[a])
        return remote(place(p, turn(-way), 0, cols), place(p, 2, 0, cols), send.at[0], onto.at[a, p], beside(p, way, core))

    def others(k, p, step):
        cols = pl.ds(begins[k], PARTS[k])
        three = pl.ds(1, SIDE - 1)
        return remote(
            place(p, three, 0, cols), place(p, three, (-step) % SIDE, cols),
            send.at[0], far.at[k, p, (1 - step) // 2], beside(1 - p, step, core),
        )

    def others_arrived(k, p, index):
        block = place(p, pl.ds(1, SIDE - 1), 0, pl.ds(begins[k], PARTS[k]))
        remote(block, block, send.at[0], far.at[k, p, index], sibling).wait_recv()

    def line_onward(k, p):
        cols = pl.ds(begins[k], PARTS[k])
        whole = pl.ds(0, SIDE)
        return remote(place(p, whole, turn(-way), cols), place(p, whole, 2, cols), send.at[0], over.at[k, p], beside(1 - p, way, core))

    zero = DEPTH - 1
    blocks = zero // REACH

    def slab_block(s):
        low = zero - REACH * s if s > 0 else zero
        return slabs.at[pl.ds(low + core * (2 * (zero - low) - REACH + 1), REACH)]

    def slab_copy(d):
        return remote(slabs.at[zero], slabs.at[zero - way * d], line_send.at[d - 1], line_got.at[d - 1], {"row": row, "col": z + way * d})

    def block_copy(s):
        i = REACH + s - 1
        return remote(slab_block(s), slab_block(s + 1), line_send.at[i], line_got.at[i], {"row": row, "col": z + way * REACH})

    def line_step(s):
        if s == 0:
            own_slab.wait_recv()
            for d in range(1, REACH + 1):
                pl.when(there(way * d))(slab_copy(d).start)
            return
        if s == 1:
            for d in range(1, REACH + 1):
                pl.when(there(-way * d))(slab_copy(d).wait_recv)
        else:
            pl.when(there(-way * REACH))(block_copy(s - 1).wait_recv)
        if s < blocks:
            pl.when(there(way * REACH))(block_copy(s).start)
        else:
            share.start()

    halves = remote(
        int_hbm.at[:, :, pl.ds(pl.multiple_of((1 - core) * half, 128), half)],
        rows.at[:, 0, 0, core], send.at[1], side.at[0], sibling,
    )
    own_slab = remote(slabs.at[zero, core], slabs.at[zero, core], send.at[2], side.at[1], sibling)
    pair_copy = remote(pair.at[core], pair.at[core], send.at[3], side.at[2], sibling)
    side_slabs = slabs.at[pl.ds(core * DEPTH, zero)]
    share = remote(side_slabs, side_slabs, send.at[4], side.at[3], sibling)

    def result(k):
        block = out_ref.at[:, pl.ds(pl.multiple_of(mine + begins[k], 128), PARTS[k])]
        return remote(stage.at[:, pl.ds(begins[k], PARTS[k])], block, send.at[5], side.at[4], sibling)

    def denominators():
        for one in fetches[2:]:
            one.wait()
        occ_count = eocc_ref.shape[0]
        levels = jnp.broadcast_to(eocc_ref[...].reshape(1, occ_count), (pairs, occ_count)).T
        spots = lax.broadcasted_iota(jnp.int32, levels.shape, 0)
        energy = [jnp.sum(jnp.where(spots == occ_ref[i : i + 1, :], levels, 0.0), axis=0, keepdims=True) for i in (0, 1)]
        pair[core] = jnp.broadcast_to(energy[0] + energy[1], (pairs, pairs)).T
        pair_copy.start()
        virtual = evir_ref[...].reshape(1, evir_ref.shape[0])
        spots = lax.broadcasted_iota(jnp.int32, virtual.shape, 1)
        count = half // virtual.shape[1]
        lead = off_ref[0] + (2 * z + core) * count
        vir[...] = jnp.concatenate(
            [jnp.sum(jnp.where(spots == lead + a, virtual, 0.0), axis=1, keepdims=True) + virtual for a in range(count)],
            axis=1,
        )

    def split_amps():
        share.wait_recv()
        pair_copy.wait_recv()
        for a in range(DEPTH):
            amps[a] = slabs[zero + a - z]
        for i, c in enumerate((core, 1 - core)):
            full = amps[:, c].reshape(pairs, amps.shape[3])
            high = full.astype(jnp.bfloat16)
            both[i * pairs : (i + 1) * pairs, :] = high
            both[(2 + i) * pairs : (3 + i) * pairs, :] = (full - high.astype(jnp.float32)).astype(jnp.bfloat16)

    def compute(k):
        cols = pl.ds(begins[k], PARTS[k])
        block = jnp.concatenate(
            [rows[p, turn(i - x), turn(j - y), :, :, cols].reshape(-1, PARTS[k]) for p in panels for i in range(SIDE) for j in range(SIDE)],
            axis=0,
        )
        high = block.astype(jnp.bfloat16)
        low = (block - high.astype(jnp.float32)).astype(jnp.bfloat16)
        head = jnp.dot(both[...], high, preferred_element_type=jnp.float32)
        tail = jnp.dot(both[: 2 * pairs, :], low, preferred_element_type=jnp.float32)
        ladder = head[: 2 * pairs] + (head[2 * pairs :] + tail)
        stage[:, cols] = ladder[pairs:] / (pair[1 - core][:, 0:1] - vir[:, cols])
        result(k).start()
        spot = pl.ds(pl.multiple_of(mine + begins[k], 128), PARTS[k])
        out_ref[:, spot] = ladder[:pairs] / (pair[core][:, 0:1] - vir[:, cols])

    def send_others(k):
        for p in panels:
            for step in (1, -1):
                others(k, p, step).start()

    def send_line_onward(k):
        if k == 1:
            for p in panels:
                own_arrived(1, p, 1, core)
        for p in panels:
            others_arrived(k, p, core)
            line_onward(k, p).start()

    def finish(k):
        if k == 1:
            for p in panels:
                own_arrived(1, p, 1, 1 - core)
        for p in panels:
            others_arrived(k, p, 1 - core)
            line_onward(k, p).wait_recv()
        compute(k)

    halves.start()
    for axis in (0, 1):
        for step in (1, -1):
            for cc in (0, 1):
                own_direct(axis, step, cc).start()
    fetches[1].wait()
    width = amp_ref.shape[2]
    for p in panels:
        slabs[zero, core, :, p * width : (p + 1) * width] = amp_ref[:, p, :]
    own_slab.start()
    fetches[0].wait()
    halves.wait_recv()
    for p in panels:
        for step in (1, -1):
            own(1, p, 0, step).start()
    for axis in (0, 1):
        own_direct_arrived(axis, core)
    for p in panels:
        onward(0, p).start()
    for p in panels:
        for step in (1, -1):
            own(1, p, 1, step).start()
    line_step(0)
    denominators()
    for axis in (0, 1):
        own_direct_arrived(axis, 1 - core)
    for p in panels:
        onward(0, p).wait_recv()
    send_others(0)
    line_step(1)
    for p in panels:
        own_arrived(1, p, 0, core)
        onward(1, p).start()
    line_step(2)
    for p in panels:
        own_arrived(1, p, 0, 1 - core)
        onward(1, p).wait_recv()
    send_others(1)
    count = len(PARTS)
    for k in range(count):
        send_line_onward(k)
        if k + 2 < count:
            send_others(k + 2)
        if k + 3 <= blocks:
            line_step(k + 3)
            if k + 3 == blocks:
                split_amps()
        if k >= 2:
            finish(k - 2)
    finish(count - 2)
    finish(count - 1)

    for block in (rows.at[:, :, 0:3], rows.at[0, 0:3, 0:2]):
        remote(block, block, send.at[0], side.at[0], sibling).wait_send()
    for one in (halves, own_slab, pair_copy, share):
        one.wait_send()
    for d in range(1, REACH + 1):
        pl.when(there(way * d))(slab_copy(d).wait_send)
    for s in range(1, blocks):
        pl.when(there(way * REACH))(block_copy(s).wait_send)
    all_results = remote(stage, out_ref.at[:, pl.ds(mine, half)], send.at[5], side.at[4], sibling)
    all_results.wait_send()
    all_results.wait_recv()


def store_kernel(src_ref, dst_ref, sems):
    count = sems.shape[0]
    height = src_ref.shape[0] // count
    copies = [
        pltpu.make_async_copy(src_ref.at[pl.ds(i * height, height)], dst_ref.at[pl.ds(i * height, height)], sems.at[i])
        for i in range(count)
    ]
    for one in copies:
        one.start()
    for one in copies:
        one.wait()


def gather_and_contract(amplitudes, integrals, occ_pairs, eps_occ, eps_vir, vir_offset, cid=0, name="gather_and_contract"):
    panels, depth, ab = integrals.shape
    mine, _, panel = amplitudes.shape
    pairs = occ_pairs.shape[0]
    cd = panels * panel
    half = ab // 2
    hbm = pl.BlockSpec(memory_space=pltpu.HBM)
    arrays = (amplitudes, integrals, occ_pairs.T, eps_occ, eps_vir)
    return pl.pallas_call(
        gather_kernel,
        out_shape=pltpu.VMEM((pairs, ab), jnp.float32),
        in_specs=[hbm] * 5 + [pl.BlockSpec(memory_space=pltpu.SMEM)],
        out_specs=pl.BlockSpec(memory_space=pltpu.VMEM),
        scratch_shapes=[
            pltpu.VMEM((panels, SIDE, SIDE, 2, depth, half), jnp.float32),
            pltpu.VMEM((2 * DEPTH - 1, 2, mine, cd), jnp.float32),
            pltpu.VMEM((DEPTH, 2, mine, cd), jnp.float32),
            pltpu.VMEM((4 * pairs, cd), jnp.bfloat16),
            pltpu.VMEM((2, pairs, pairs), jnp.float32),
            pltpu.VMEM((1, half), jnp.float32),
            pltpu.VMEM((pairs, half), jnp.float32),
            pltpu.VMEM(amplitudes.shape, jnp.float32),
            pltpu.VMEM((2, pairs), jnp.int32),
            pltpu.VMEM(eps_occ.shape, jnp.float32),
            pltpu.VMEM(eps_vir.shape, jnp.float32),
            pltpu.SemaphoreType.DMA((5,)),
            pltpu.SemaphoreType.DMA((6,)),
            pltpu.SemaphoreType.DMA((len(PIECES), 2, 2, 2)),
            pltpu.SemaphoreType.DMA((len(PIECES), 2)),
            pltpu.SemaphoreType.DMA((len(PARTS), 2, 2)),
            pltpu.SemaphoreType.DMA((len(PARTS), 2)),
            pltpu.SemaphoreType.DMA((2 * REACH + 1,)),
            pltpu.SemaphoreType.DMA((2 * REACH + 1,)),
            pltpu.SemaphoreType.DMA((5,)),
        ],
        compiler_params=pltpu.CompilerParams(
            collective_id=cid, has_side_effects=True, vmem_limit_bytes=40 * 1024 * 1024
        ),
        cost_estimate=pl.CostEstimate(
            flops=2 * pairs * cd * ab * 3, bytes_accessed=4 * (pairs * ab + panels * depth * ab), transcendentals=0
        ),
        name=name,
    )(*(pltpu.with_memory_space_constraint(a, pltpu.HBM) for a in arrays), vir_offset)


def shards(amplitudes, integrals, occ_pairs, eps_occ, eps_vir, vir_offset):
    update = gather_and_contract(amplitudes, integrals, occ_pairs, eps_occ, eps_vir, vir_offset)
    return pl.pallas_call(
        store_kernel,
        out_shape=jax.ShapeDtypeStruct(update.shape, jnp.float32),
        in_specs=[pl.BlockSpec(memory_space=pltpu.VMEM)],
        out_specs=pl.BlockSpec(memory_space=pl.ANY),
        scratch_shapes=[pltpu.SemaphoreType.DMA((8,))],
        cost_estimate=pl.CostEstimate(flops=0, bytes_accessed=4 * update.size, transcendentals=0),
        name="store",
    )(pltpu.with_memory_space_constraint(update, pltpu.VMEM))


def solution(mesh):
    return jax.shard_map(
        shards,
        mesh=mesh,
        in_specs=(
            P(("row", "col"), None, None),
            P(None, "row", "col"),
            P("row", None),
            P(),
            P(),
            P(),
        ),
        out_specs=P("row", "col"),
        check_vma=False,
    )
```

time: 164 us -> 61.2 us (0.37)
  the two profiles are of different devices: /device:TPU:1 before, /device:TPU:35 now
where the time goes in v3:
time: 61.2 us; the launch traced here: 61.1 us
  Pallas kernels  60.5 us (99%)
  between operations  0.66 us (1%)
    pallas_call x1, Pallas kernels, gather_and_contract(): pl.pallas_call(gather_kernel, out_shape=pltpu.VMEM((pairs, ab), jnp.float...  58.7 us
    pallas_call x1, Pallas kernels, shards(): pl.pallas_call(store_kernel, out_shape=jax.ShapeDtypeStruct(update.shape,...  1.77 us

profile of v3, /device:TPU:35, one launch (start us, length us, event | category | flops | bytes accessed | tf_op | source)
XLA Modules:
  0.0 61.1 jit_solution(16781823238491634951)
XLA Ops:
  0.7 58.7 %gather_and_contract.1.src_ref = f32[128,6400]{1,0:T(8,128)S(1)} custom-call(f32[8,2,256]{2,1,0:T(2,128)} %amp_hbm.1, f32[2,8,6400]{2,1,0:T(8,128)} %int_hbm.1, s32[2,128]{1,0:T(2,128)} %bitcast.1, f32[200]{0:T(256)} %eocc_hbm.1, f32[800]{0:T(1024)} %evir_hbm.1, s32[1]{0:T(128)S(6)} %copy.7.off_ref), custom_call_target="tpu_custom_call" | custom-call | flops 2516582400 | bytes 3686400 | tf_op jit(solution)/shard_map/gather_and_contract/pallas_call | solution.py:327
  59.3 1.8 %store.1 = f32[128,6400]{1,0:T(8,128)} custom-call(f32[128,6400]{1,0:T(8,128)S(1)} %gather_and_contract.1.src_ref), custom_call_target="tpu_custom_call" | custom-call | bytes 3276800 | tf_op jit(solution)/shard_map/store/pallas_call | solution.py:366

commit v4 on v3

--- a/solution.py
+++ b/solution.py
@@ -11,15 +11,17 @@
 SIDE = 4
 DEPTH = 16
 REACH = 3
+LAST = 4
 PIECES = (640, 2560)
 PARTS = (640, 768, 768, 640, 384)
+POINTS = (0, 1, 2, 3, 4)
 
 
 def gather_kernel(
     amp_hbm, int_hbm, occ_hbm, eocc_hbm, evir_hbm, off_ref, out_ref,
     rows, slabs, amps, both, pair, vir, stage,
     amp_ref, occ_ref, eocc_ref, evir_ref,
-    local, send, near, onto, far, over, line_send, line_got, side,
+    local, send, near, onto, far, over, line_send, line_got, side, ready,
 ):
     row, z = lax.axis_index("row"), lax.axis_index("col")
     x, y, core = row // 8, (row // 2) % SIDE, row % 2
@@ -39,8 +41,42 @@
 
     sibling = {"row": row + way, "col": z}
 
-    def there(d):
-        return jnp.logical_and(z + d >= 0, z + d < DEPTH)
+    zero = DEPTH - 1
+    blocks = zero // REACH
+
+    def down_blocks(v):
+        return jnp.where(v + 2 * REACH <= zero, 2, 1)
+
+    def blocks_at(v):
+        return jnp.where(core == 0, blocks - down_blocks(v), down_blocks(v))
+
+    def on_line(d):
+        return {"row": row, "col": (z + d + DEPTH) % DEPTH}
+
+    def target(d):
+        return z + way * d
+
+    def sends(d, count):
+        inside = jnp.logical_or(core == 0, target(d) >= 0)
+        return jnp.logical_and(inside, blocks_at((target(d) + DEPTH) % DEPTH) >= count)
+
+    def sends_slab(d):
+        return sends(d, 1)
+
+    def gets_slab(d):
+        return jnp.logical_or(core == 0, z + d <= zero)
+
+    def seam_to(d):
+        return jnp.logical_and(core == 1, z < d)
+
+    def seam_from(d):
+        return jnp.logical_and(core == 1, z + d > zero)
+
+    def sends_block(s):
+        return sends(REACH, s + 1)
+
+    def gets_block(s):
+        return blocks_at(z) >= s + 1
 
     def fetch(i, src, dst):
         return pltpu.make_async_copy(src, dst, local.at[i])
@@ -67,10 +103,16 @@
             for cc in (0, 1):
                 greet(beside(axis, step, cc))
     for d in range(1, REACH + 1):
-        for dd in (d, -d):
-            pl.when(there(dd))(functools.partial(greet, {"row": row, "col": z + dd}))
-            greeted = greeted + there(dd).astype(jnp.int32)
+        pl.when(gets_slab(d))(functools.partial(greet, on_line(-way * d)))
+        pl.when(seam_to(d))(functools.partial(greet, on_line(way * d)))
+        greeted = greeted + sends_slab(d).astype(jnp.int32) + seam_from(d).astype(jnp.int32)
     pl.semaphore_wait(barrier, greeted)
+
+    def tell(to):
+        pl.semaphore_signal(ready, inc=1, device_id=to, device_id_type=MESH)
+
+    for d in range(1, REACH + 1):
+        pl.when(seam_from(d))(functools.partial(tell, on_line(-way * d)))
 
     def remote(src, dst, sent, got, to):
         return pltpu.make_async_remote_copy(
@@ -128,34 +170,38 @@
         whole = pl.ds(0, SIDE)
         return remote(place(p, whole, turn(-way), cols), place(p, whole, 2, cols), send.at[0], over.at[k, p], beside(1 - p, way, core))
 
-    zero = DEPTH - 1
-    blocks = zero // REACH
-
     def slab_block(s):
         low = zero - REACH * s if s > 0 else zero
         return slabs.at[pl.ds(low + core * (2 * (zero - low) - REACH + 1), REACH)]
 
     def slab_copy(d):
-        return remote(slabs.at[zero], slabs.at[zero - way * d], line_send.at[d - 1], line_got.at[d - 1], {"row": row, "col": z + way * d})
+        return remote(slabs.at[zero], slabs.at[zero - way * d], line_send.at[d - 1], line_got.at[d - 1], on_line(way * d))
 
     def block_copy(s):
         i = REACH + s - 1
-        return remote(slab_block(s), slab_block(s + 1), line_send.at[i], line_got.at[i], {"row": row, "col": z + way * REACH})
+        return remote(slab_block(s), slab_block(s + 1), line_send.at[i], line_got.at[i], on_line(way * REACH))
 
     def line_step(s):
         if s == 0:
             own_slab.wait_recv()
             for d in range(1, REACH + 1):
-                pl.when(there(way * d))(slab_copy(d).start)
+                pl.when(sends_slab(d))(slab_copy(d).start)
             return
         if s == 1:
             for d in range(1, REACH + 1):
-                pl.when(there(-way * d))(slab_copy(d).wait_recv)
+                pl.when(gets_slab(d))(slab_copy(d).wait_recv)
         else:
-            pl.when(there(-way * REACH))(block_copy(s - 1).wait_recv)
-        if s < blocks:
-            pl.when(there(way * REACH))(block_copy(s).start)
+            pl.when(gets_block(s - 1))(block_copy(s - 1).wait_recv)
+        if s == 2:
+            late = sum(seam_to(d).astype(jnp.int32) for d in range(1, REACH + 1))
+            pl.when(late > 0)(functools.partial(pl.semaphore_wait, ready, late))
+            for d in range(1, REACH + 1):
+                pl.when(seam_to(d))(slab_copy(d).start)
+        if s < LAST:
+            pl.when(sends_block(s))(block_copy(s).start)
         else:
+            for d in range(1, REACH + 1):
+                pl.when(seam_from(d))(slab_copy(d).wait_recv)
             share.start()
 
     halves = remote(
@@ -193,7 +239,8 @@
         share.wait_recv()
         pair_copy.wait_recv()
         for a in range(DEPTH):
-            amps[a] = slabs[zero + a - z]
+            ahead = (a - z + DEPTH) % DEPTH
+            amps[a] = slabs[jnp.where(ahead <= REACH * down_blocks(z), zero + ahead, ahead - 1)]
         for i, c in enumerate((core, 1 - core)):
             full = amps[:, c].reshape(pairs, amps.shape[3])
             high = full.astype(jnp.bfloat16)
@@ -260,44 +307,55 @@
     for p in panels:
         for step in (1, -1):
             own(1, p, 1, step).start()
-    line_step(0)
+
+    def line_point(point):
+        for s in range(LAST + 1):
+            if POINTS[s] == point:
+                line_step(s)
+
+    line_point(0)
     denominators()
     for axis in (0, 1):
         own_direct_arrived(axis, 1 - core)
     for p in panels:
         onward(0, p).wait_recv()
     send_others(0)
-    line_step(1)
     for p in panels:
         own_arrived(1, p, 0, core)
         onward(1, p).start()
-    line_step(2)
+    line_point(1)
+    send_line_onward(0)
     for p in panels:
         own_arrived(1, p, 0, 1 - core)
         onward(1, p).wait_recv()
     send_others(1)
+    line_point(2)
     count = len(PARTS)
-    for k in range(count):
+    finished = 0
+    send_others(2)
+    for k in range(1, count):
         send_line_onward(k)
         if k + 2 < count:
             send_others(k + 2)
-        if k + 3 <= blocks:
-            line_step(k + 3)
-            if k + 3 == blocks:
-                split_amps()
-        if k >= 2:
-            finish(k - 2)
-    finish(count - 2)
-    finish(count - 1)
+        line_point(k + 2)
+        if k + 2 == POINTS[LAST]:
+            split_amps()
+        if k + 2 >= POINTS[LAST]:
+            while finished <= k - 2:
+                finish(finished)
+                finished += 1
+    while finished < count:
+        finish(finished)
+        finished += 1
 
     for block in (rows.at[:, :, 0:3], rows.at[0, 0:3, 0:2]):
         remote(block, block, send.at[0], side.at[0], sibling).wait_send()
     for one in (halves, own_slab, pair_copy, share):
         one.wait_send()
     for d in range(1, REACH + 1):
-        pl.when(there(way * d))(slab_copy(d).wait_send)
-    for s in range(1, blocks):
-        pl.when(there(way * REACH))(block_copy(s).wait_send)
+        pl.when(jnp.logical_or(sends_slab(d), seam_to(d)))(slab_copy(d).wait_send)
+    for s in range(1, LAST):
+        pl.when(sends_block(s))(block_copy(s).wait_send)
     all_results = remote(stage, out_ref.at[:, pl.ds(mine, half)], send.at[5], side.at[4], sibling)
     all_results.wait_send()
     all_results.wait_recv()
@@ -347,9 +405,10 @@
             pltpu.SemaphoreType.DMA((len(PIECES), 2)),
             pltpu.SemaphoreType.DMA((len(PARTS), 2, 2)),
             pltpu.SemaphoreType.DMA((len(PARTS), 2)),
-            pltpu.SemaphoreType.DMA((2 * REACH + 1,)),
-            pltpu.SemaphoreType.DMA((2 * REACH + 1,)),
+            pltpu.SemaphoreType.DMA((REACH + LAST - 1,)),
+            pltpu.SemaphoreType.DMA((REACH + LAST - 1,)),
             pltpu.SemaphoreType.DMA((5,)),
+            pltpu.SemaphoreType.REGULAR,
         ],
         compiler_params=pltpu.CompilerParams(
             collective_id=cid, has_side_effects=True, vmem_limit_bytes=40 * 1024 * 1024

time: 61.2 us -> 53.8 us (0.88)
  the two profiles are of different devices: /device:TPU:35 before, /device:TPU:1 now
where the time goes in v4:
time: 53.8 us; the launch traced here: 53.6 us
  Pallas kernels  53 us (99%)
  between operations  0.66 us (1%)
    pallas_call x1, Pallas kernels, gather_and_contract(): pl.pallas_call(gather_kernel, out_shape=pltpu.VMEM((pairs, ab), jnp.float...  51.2 us
    pallas_call x1, Pallas kernels, shards(): pl.pallas_call(store_kernel, out_shape=jax.ShapeDtypeStruct(update.shape,...  1.77 us

profile of v4, /device:TPU:1, one launch (start us, length us, event | category | flops | bytes accessed | tf_op | source)
XLA Modules:
  0.0 53.6 jit_solution(9637006564380256085)
XLA Ops:
  0.7 51.2 %gather_and_contract.1.src_ref = f32[128,6400]{1,0:T(8,128)S(1)} custom-call(f32[8,2,256]{2,1,0:T(2,128)} %amp_hbm.1, f32[2,8,6400]{2,1,0:T(8,128)} %int_hbm.1, s32[2,128]{1,0:T(2,128)} %bitcast.1, f32[200]{0:T(256)} %eocc_hbm.1, f32[800]{0:T(1024)} %evir_hbm.1, s32[1]{0:T(128)S(6)} %copy.7.off_ref), custom_call_target="tpu_custom_call" | custom-call | flops 2516582400 | bytes 3686400 | tf_op jit(solution)/shard_map/gather_and_contract/pallas_call | solution.py:385
  51.9 1.8 %store.1 = f32[128,6400]{1,0:T(8,128)} custom-call(f32[128,6400]{1,0:T(8,128)S(1)} %gather_and_contract.1.src_ref), custom_call_target="tpu_custom_call" | custom-call | bytes 3276800 | tf_op jit(solution)/shard_map/store/pallas_call | solution.py:425

commit v5 on v4

--- a/solution.py
+++ b/solution.py
@@ -13,13 +13,13 @@
 REACH = 3
 LAST = 4
 PIECES = (640, 2560)
-PARTS = (640, 768, 768, 640, 384)
+PARTS = (640, 1024, 1024, 512)
 POINTS = (0, 1, 2, 3, 4)
 
 
 def gather_kernel(
     amp_hbm, int_hbm, occ_hbm, eocc_hbm, evir_hbm, off_ref, out_ref,
-    rows, slabs, amps, both, pair, vir, stage,
+    shard, rows, slabs, amps, both, pair, vir, stage,
     amp_ref, occ_ref, eocc_ref, evir_ref,
     local, send, near, onto, far, over, line_send, line_got, side, ready,
 ):
@@ -82,7 +82,7 @@
         return pltpu.make_async_copy(src, dst, local.at[i])
 
     fetches = [
-        fetch(0, int_hbm.at[:, :, pl.ds(mine, half)], rows.at[:, 0, 0, core]),
+        fetch(0, int_hbm, shard),
         fetch(1, amp_hbm, amp_ref),
         fetch(2, occ_hbm, occ_ref),
         fetch(3, eocc_hbm, eocc_ref),
@@ -128,7 +128,7 @@
         return rows.at[1, along_second, along_first, :, :, cols]
 
     def own_direct(axis, step, cc):
-        src = int_hbm.at[:, :, pl.ds(pl.multiple_of(cc * half, 128), PIECES[0])]
+        src = shard.at[:, :, pl.ds(pl.multiple_of(cc * half, 128), PIECES[0])]
         back = (-step) % SIDE
         spot = (slice(None), back, 0) if axis == 0 else (slice(None), 0, back)
         dst = rows.at[(*spot, core, slice(None), pl.ds(0, PIECES[0]))]
@@ -205,7 +205,7 @@
             share.start()
 
     halves = remote(
-        int_hbm.at[:, :, pl.ds(pl.multiple_of((1 - core) * half, 128), half)],
+        shard.at[:, :, pl.ds(pl.multiple_of((1 - core) * half, 128), half)],
         rows.at[:, 0, 0, core], send.at[1], side.at[0], sibling,
     )
     own_slab = remote(slabs.at[zero, core], slabs.at[zero, core], send.at[2], side.at[1], sibling)
@@ -285,17 +285,21 @@
             line_onward(k, p).wait_recv()
         compute(k)
 
-    halves.start()
+    fetches[0].wait()
     for axis in (0, 1):
         for step in (1, -1):
             for cc in (0, 1):
                 own_direct(axis, step, cc).start()
+        if axis == 0:
+            halves.start()
+    keep = pltpu.make_async_copy(shard.at[:, :, pl.ds(mine, half)], rows.at[:, 0, 0, core], local.at[0])
+    keep.start()
     fetches[1].wait()
     width = amp_ref.shape[2]
     for p in panels:
         slabs[zero, core, :, p * width : (p + 1) * width] = amp_ref[:, p, :]
     own_slab.start()
-    fetches[0].wait()
+    keep.wait()
     halves.wait_recv()
     for p in panels:
         for step in (1, -1):
@@ -388,6 +392,7 @@
         in_specs=[hbm] * 5 + [pl.BlockSpec(memory_space=pltpu.SMEM)],
         out_specs=pl.BlockSpec(memory_space=pltpu.VMEM),
         scratch_shapes=[
+            pltpu.VMEM(integrals.shape, jnp.float32),
             pltpu.VMEM((panels, SIDE, SIDE, 2, depth, half), jnp.float32),
             pltpu.VMEM((2 * DEPTH - 1, 2, mine, cd), jnp.float32),
             pltpu.VMEM((DEPTH, 2, mine, cd), jnp.float32),

time: 53.8 us -> 51.4 us (0.955)
  Pallas kernels: 53 us -> 50.6 us
    pallas_call x1, Pallas kernels: 51.2 us -> 48.8 us  [gather_and_contract(): pl.pallas_call(gather_kernel, out_shape=pltpu.VMEM((pairs, ab), jnp.float...]
where the time goes in v5:
time: 51.4 us; the launch traced here: 51.3 us
  Pallas kernels  50.6 us (98%)
  between operations  0.66 us (1%)
    pallas_call x1, Pallas kernels, gather_and_contract(): pl.pallas_call(gather_kernel, out_shape=pltpu.VMEM((pairs, ab), jnp.float...  48.8 us
    pallas_call x1, Pallas kernels, shards(): pl.pallas_call(store_kernel, out_shape=jax.ShapeDtypeStruct(update.shape,...  1.77 us

profile of v5, /device:TPU:1, one launch (start us, length us, event | category | flops | bytes accessed | tf_op | source)
XLA Modules:
  0.0 51.3 jit_solution(7158823431337498653)
XLA Ops:
  0.7 48.8 %gather_and_contract.1.src_ref = f32[128,6400]{1,0:T(8,128)S(1)} custom-call(f32[8,2,256]{2,1,0:T(2,128)} %amp_hbm.1, f32[2,8,6400]{2,1,0:T(8,128)} %int_hbm.1, s32[2,128]{1,0:T(2,128)} %bitcast.1, f32[200]{0:T(256)} %eocc_hbm.1, f32[800]{0:T(1024)} %evir_hbm.1, s32[1]{0:T(128)S(6)} %copy.7.off_ref), custom_call_target="tpu_custom_call" | custom-call | flops 2516582400 | bytes 3686400 | tf_op jit(solution)/shard_map/gather_and_contract/pallas_call | solution.py:389
  49.5 1.8 %store.1 = f32[128,6400]{1,0:T(8,128)} custom-call(f32[128,6400]{1,0:T(8,128)S(1)} %gather_and_contract.1.src_ref), custom_call_target="tpu_custom_call" | custom-call | bytes 3276800 | tf_op jit(solution)/shard_map/store/pallas_call | solution.py:430

commit v6 on v5

--- a/solution.py
+++ b/solution.py
@@ -10,11 +10,12 @@
 MESH = pl.DeviceIdType.MESH
 SIDE = 4
 DEPTH = 16
-REACH = 3
-LAST = 4
+REACH = 4
+LAST = 3
+GATE = 8
 PIECES = (640, 2560)
 PARTS = (640, 1024, 1024, 512)
-POINTS = (0, 1, 2, 3, 4)
+POINTS = (0, 1, 2, 4)
 
 
 def gather_kernel(
@@ -42,7 +43,7 @@
     sibling = {"row": row + way, "col": z}
 
     zero = DEPTH - 1
-    blocks = zero // REACH
+    blocks = -(-zero // REACH)
 
     def down_blocks(v):
         return jnp.where(v + 2 * REACH <= zero, 2, 1)
@@ -53,30 +54,25 @@
     def on_line(d):
         return {"row": row, "col": (z + d + DEPTH) % DEPTH}
 
-    def target(d):
-        return z + way * d
-
-    def sends(d, count):
-        inside = jnp.logical_or(core == 0, target(d) >= 0)
-        return jnp.logical_and(inside, blocks_at((target(d) + DEPTH) % DEPTH) >= count)
-
-    def sends_slab(d):
-        return sends(d, 1)
-
-    def gets_slab(d):
-        return jnp.logical_or(core == 0, z + d <= zero)
-
-    def seam_to(d):
-        return jnp.logical_and(core == 1, z < d)
-
-    def seam_from(d):
-        return jnp.logical_and(core == 1, z + d > zero)
+    def gated(v, d):
+        first = jnp.logical_and(v == 0, row == 0)
+        up = jnp.logical_and(jnp.logical_and(v >= 0, v < GATE), jnp.logical_and(v + d <= zero, jnp.logical_not(first)))
+        return jnp.where(core == 0, up, jnp.logical_and(v < d, v >= 0))
+
+    def gated_to(d):
+        return gated(z, d)
+
+    def gated_from(d):
+        return gated(jnp.where(core == 0, z - d, (z + d) % DEPTH), d)
 
     def sends_block(s):
-        return sends(REACH, s + 1)
+        inside = jnp.logical_or(core == 0, z >= REACH)
+        return jnp.logical_and(inside, blocks_at((z + way * REACH + DEPTH) % DEPTH) > s)
 
     def gets_block(s):
-        return blocks_at(z) >= s + 1
+        return blocks_at(z) > s
+
+    relays = jnp.logical_and(core == 0, sends_block(2))
 
     def fetch(i, src, dst):
         return pltpu.make_async_copy(src, dst, local.at[i])
@@ -103,16 +99,16 @@
             for cc in (0, 1):
                 greet(beside(axis, step, cc))
     for d in range(1, REACH + 1):
-        pl.when(gets_slab(d))(functools.partial(greet, on_line(-way * d)))
-        pl.when(seam_to(d))(functools.partial(greet, on_line(way * d)))
-        greeted = greeted + sends_slab(d).astype(jnp.int32) + seam_from(d).astype(jnp.int32)
+        pl.when(gated_to(d))(functools.partial(greet, on_line(way * d)))
+        pl.when(jnp.logical_not(gated_from(d)))(functools.partial(greet, on_line(-way * d)))
+        greeted = greeted + gated_from(d).astype(jnp.int32) + 1 - gated_to(d).astype(jnp.int32)
     pl.semaphore_wait(barrier, greeted)
 
     def tell(to):
         pl.semaphore_signal(ready, inc=1, device_id=to, device_id_type=MESH)
 
     for d in range(1, REACH + 1):
-        pl.when(seam_from(d))(functools.partial(tell, on_line(-way * d)))
+        pl.when(gated_from(d))(functools.partial(tell, on_line(-way * d)))
 
     def remote(src, dst, sent, got, to):
         return pltpu.make_async_remote_copy(
@@ -181,27 +177,31 @@
         i = REACH + s - 1
         return remote(slab_block(s), slab_block(s + 1), line_send.at[i], line_got.at[i], on_line(way * REACH))
 
+    def send_gated():
+        late = sum(gated_to(d).astype(jnp.int32) for d in range(1, REACH + 1))
+        pl.when(late > 0)(functools.partial(pl.semaphore_wait, ready, late))
+        for d in range(1, REACH + 1):
+            pl.when(gated_to(d))(slab_copy(d).start)
+
     def line_step(s):
         if s == 0:
             own_slab.wait_recv()
             for d in range(1, REACH + 1):
-                pl.when(sends_slab(d))(slab_copy(d).start)
-            return
+                pl.when(jnp.logical_not(gated_to(d)))(slab_copy(d).start)
+            pl.when(core == 0)(send_gated)
         if s == 1:
             for d in range(1, REACH + 1):
-                pl.when(gets_slab(d))(slab_copy(d).wait_recv)
-        else:
-            pl.when(gets_block(s - 1))(block_copy(s - 1).wait_recv)
+                pl.when(jnp.logical_or(core == 0, z + d <= zero))(slab_copy(d).wait_recv)
+            pl.when(sends_block(1))(block_copy(1).start)
         if s == 2:
-            late = sum(seam_to(d).astype(jnp.int32) for d in range(1, REACH + 1))
-            pl.when(late > 0)(functools.partial(pl.semaphore_wait, ready, late))
+            pl.when(core == 1)(send_gated)
+            pl.when(relays)(block_copy(1).wait_recv)
+            pl.when(sends_block(2))(block_copy(2).start)
+        if s == LAST:
+            pl.when(jnp.logical_and(gets_block(1), jnp.logical_not(relays)))(block_copy(1).wait_recv)
+            pl.when(gets_block(2))(block_copy(2).wait_recv)
             for d in range(1, REACH + 1):
-                pl.when(seam_to(d))(slab_copy(d).start)
-        if s < LAST:
-            pl.when(sends_block(s))(block_copy(s).start)
-        else:
-            for d in range(1, REACH + 1):
-                pl.when(seam_from(d))(slab_copy(d).wait_recv)
+                pl.when(jnp.logical_and(core == 1, z + d > zero))(slab_copy(d).wait_recv)
             share.start()
 
     halves = remote(
@@ -210,7 +210,8 @@
     )
     own_slab = remote(slabs.at[zero, core], slabs.at[zero, core], send.at[2], side.at[1], sibling)
     pair_copy = remote(pair.at[core], pair.at[core], send.at[3], side.at[2], sibling)
-    side_slabs = slabs.at[pl.ds(core * DEPTH, zero)]
+    reach = REACH * LAST
+    side_slabs = slabs.at[pl.ds(zero - reach + core * (reach + 1), reach)]
     share = remote(side_slabs, side_slabs, send.at[4], side.at[3], sibling)
 
     def result(k):
@@ -327,8 +328,8 @@
     for p in panels:
         own_arrived(1, p, 0, core)
         onward(1, p).start()
+    send_line_onward(0)
     line_point(1)
-    send_line_onward(0)
     for p in panels:
         own_arrived(1, p, 0, 1 - core)
         onward(1, p).wait_recv()
@@ -357,7 +358,7 @@
     for one in (halves, own_slab, pair_copy, share):
         one.wait_send()
     for d in range(1, REACH + 1):
-        pl.when(jnp.logical_or(sends_slab(d), seam_to(d)))(slab_copy(d).wait_send)
+        slab_copy(d).wait_send()
     for s in range(1, LAST):
         pl.when(sends_block(s))(block_copy(s).wait_send)
     all_results = remote(stage, out_ref.at[:, pl.ds(mine, half)], send.at[5], side.at[4], sibling)

time: 51.4 us -> 50.5 us (0.982)
  Pallas kernels: 50.6 us -> 49.7 us
    pallas_call x1, Pallas kernels: 48.8 us -> 48 us  [gather_and_contract(): pl.pallas_call(gather_kernel, out_shape=pltpu.VMEM((pairs, ab), jnp.float...]
where the time goes in v6:
time: 50.5 us; the launch traced here: 50.4 us
  Pallas kernels  49.7 us (98%)
  between operations  0.66 us (1%)
    pallas_call x1, Pallas kernels, gather_and_contract(): pl.pallas_call(gather_kernel, out_shape=pltpu.VMEM((pairs, ab), jnp.float...  48 us
    pallas_call x1, Pallas kernels, shards(): pl.pallas_call(store_kernel, out_shape=jax.ShapeDtypeStruct(update.shape,...  1.77 us

profile of v6, /device:TPU:1, one launch (start us, length us, event | category | flops | bytes accessed | tf_op | source)
XLA Modules:
  0.0 50.4 jit_solution(7500106984478729797)
XLA Ops:
  0.7 48.0 %gather_and_contract.1.src_ref = f32[128,6400]{1,0:T(8,128)S(1)} custom-call(f32[8,2,256]{2,1,0:T(2,128)} %amp_hbm.1, f32[2,8,6400]{2,1,0:T(8,128)} %int_hbm.1, s32[2,128]{1,0:T(2,128)} %bitcast.1, f32[200]{0:T(256)} %eocc_hbm.1, f32[800]{0:T(1024)} %evir_hbm.1, s32[1]{0:T(128)S(6)} %copy.7.off_ref), custom_call_target="tpu_custom_call" | custom-call | flops 2516582400 | bytes 3686400 | tf_op jit(solution)/shard_map/gather_and_contract/pallas_call | solution.py:390
  48.6 1.8 %store.1 = f32[128,6400]{1,0:T(8,128)} custom-call(f32[128,6400]{1,0:T(8,128)S(1)} %gather_and_contract.1.src_ref), custom_call_target="tpu_custom_call" | custom-call | bytes 3276800 | tf_op jit(solution)/shard_map/store/pallas_call | solution.py:431

commit v7 on v6

--- a/solution.py
+++ b/solution.py
@@ -13,6 +13,7 @@
 REACH = 4
 LAST = 3
 GATE = 8
+SOON = 6
 PIECES = (640, 2560)
 PARTS = (640, 1024, 1024, 512)
 POINTS = (0, 1, 2, 4)
@@ -22,7 +23,7 @@
     amp_hbm, int_hbm, occ_hbm, eocc_hbm, evir_hbm, off_ref, out_ref,
     shard, rows, slabs, amps, both, pair, vir, stage,
     amp_ref, occ_ref, eocc_ref, evir_ref,
-    local, send, near, onto, far, over, line_send, line_got, side, ready,
+    local, send, near, onto, far, over, line_send, line_got, side, ready, awake,
 ):
     row, z = lax.axis_index("row"), lax.axis_index("col")
     x, y, core = row // 8, (row // 2) % SIDE, row % 2
@@ -72,6 +73,7 @@
     def gets_block(s):
         return blocks_at(z) > s
 
+    after = z >= GATE
     relays = jnp.logical_and(core == 0, sends_block(2))
 
     def fetch(i, src, dst):
@@ -92,12 +94,21 @@
     def greet(to):
         pl.semaphore_signal(barrier, inc=1, device_id=to, device_id_type=MESH)
 
-    greeted = 9
-    greet(sibling)
-    for axis in (0, 1):
-        for step in (1, -1):
-            for cc in (0, 1):
-                greet(beside(axis, step, cc))
+    latest = jnp.logical_and(row == 0, z == 0)
+
+    def is_latest(to):
+        return jnp.logical_and(to["row"] == 0, z == 0)
+
+    by_side = is_latest(sibling)
+    next_to = functools.reduce(jnp.logical_or, [is_latest(beside(axis, step, 0)) for axis in (0, 1) for step in (1, -1)])
+    greeted = 9 - jnp.logical_or(by_side, next_to).astype(jnp.int32)
+    around = [sibling] + [beside(axis, step, cc) for axis in (0, 1) for step in (1, -1) for cc in (0, 1)]
+
+    @pl.when(jnp.logical_not(latest))
+    def _():
+        for to in around:
+            greet(to)
+
     for d in range(1, REACH + 1):
         pl.when(gated_to(d))(functools.partial(greet, on_line(way * d)))
         pl.when(jnp.logical_not(gated_from(d)))(functools.partial(greet, on_line(-way * d)))
@@ -109,6 +120,11 @@
 
     for d in range(1, REACH + 1):
         pl.when(gated_from(d))(functools.partial(tell, on_line(-way * d)))
+
+    @pl.when(latest)
+    def _():
+        for to in around:
+            pl.semaphore_signal(awake, inc=1, device_id=to, device_id_type=MESH)
 
     def remote(src, dst, sent, got, to):
         return pltpu.make_async_remote_copy(
@@ -286,39 +302,66 @@
             line_onward(k, p).wait_recv()
         compute(k)
 
+    ways = [(axis, step) for axis in (0, 1) for step in (1, -1)]
+
+    def start_direct(held):
+        for axis, step in ways:
+            for cc in (0, 1):
+                pl.when(is_latest(beside(axis, step, cc)) == held)(own_direct(axis, step, cc).start)
+
+    def start_own(phase, held):
+        for p in panels:
+            for step in (1, -1):
+                axis = phase if p == 0 else 1 - phase
+                pl.when(is_latest(beside(axis, step, core)) == held)(own(1, p, phase, step).start)
+
     fetches[0].wait()
-    for axis in (0, 1):
-        for step in (1, -1):
-            for cc in (0, 1):
-                own_direct(axis, step, cc).start()
-        if axis == 0:
-            halves.start()
+    start_direct(False)
+    pl.when(jnp.logical_not(by_side))(halves.start)
     keep = pltpu.make_async_copy(shard.at[:, :, pl.ds(mine, half)], rows.at[:, 0, 0, core], local.at[0])
     keep.start()
     fetches[1].wait()
     width = amp_ref.shape[2]
     for p in panels:
         slabs[zero, core, :, p * width : (p + 1) * width] = amp_ref[:, p, :]
-    own_slab.start()
+    pl.when(jnp.logical_not(by_side))(own_slab.start)
+
+    @pl.when(by_side)
+    def _():
+        pl.semaphore_wait(awake, 1)
+        halves.start()
+        own_slab.start()
+
     keep.wait()
     halves.wait_recv()
-    for p in panels:
-        for step in (1, -1):
-            own(1, p, 0, step).start()
+    start_own(0, False)
+    pl.when(after)(functools.partial(line_step, 0))
+
+    @pl.when(next_to)
+    def _():
+        start_own(1, False)
+        pl.semaphore_wait(awake, 1)
+        start_direct(True)
+        start_own(0, True)
+        start_own(1, True)
+
     for axis in (0, 1):
         own_direct_arrived(axis, core)
     for p in panels:
         onward(0, p).start()
-    for p in panels:
-        for step in (1, -1):
-            own(1, p, 1, step).start()
+
+    @pl.when(jnp.logical_not(next_to))
+    def _():
+        for p in panels:
+            for step in (1, -1):
+                own(1, p, 1, step).start()
 
     def line_point(point):
-        for s in range(LAST + 1):
+        for s in range(2, LAST + 1):
             if POINTS[s] == point:
                 line_step(s)
 
-    line_point(0)
+    pl.when(jnp.logical_not(after))(functools.partial(line_step, 0))
     denominators()
     for axis in (0, 1):
         own_direct_arrived(axis, 1 - core)
@@ -328,8 +371,9 @@
     for p in panels:
         own_arrived(1, p, 0, core)
         onward(1, p).start()
+    pl.when(z >= SOON)(functools.partial(line_step, 1))
     send_line_onward(0)
-    line_point(1)
+    pl.when(z < SOON)(functools.partial(line_step, 1))
     for p in panels:
         own_arrived(1, p, 0, 1 - core)
         onward(1, p).wait_recv()
@@ -415,6 +459,7 @@
             pltpu.SemaphoreType.DMA((REACH + LAST - 1,)),
             pltpu.SemaphoreType.DMA((5,)),
             pltpu.SemaphoreType.REGULAR,
+            pltpu.SemaphoreType.REGULAR,
         ],
         compiler_params=pltpu.CompilerParams(
             collective_id=cid, has_side_effects=True, vmem_limit_bytes=40 * 1024 * 1024

time: 50.5 us -> 49.9 us (0.988)
  Pallas kernels: 49.7 us -> 49.1 us
    pallas_call x1, Pallas kernels: 48 us -> 47.4 us  [gather_and_contract(): pl.pallas_call(gather_kernel, out_shape=pltpu.VMEM((pairs, ab), jnp.float...]
where the time goes in v7:
time: 49.9 us; the launch traced here: 49.8 us
  Pallas kernels  49.1 us (98%)
  between operations  0.66 us (1%)
    pallas_call x1, Pallas kernels, gather_and_contract(): pl.pallas_call(gather_kernel, out_shape=pltpu.VMEM((pairs, ab), jnp.float...  47.4 us
    pallas_call x1, Pallas kernels, shards(): pl.pallas_call(store_kernel, out_shape=jax.ShapeDtypeStruct(update.shape,...  1.77 us

profile of v7, /device:TPU:1, one launch (start us, length us, event | category | flops | bytes accessed | tf_op | source)
XLA Modules:
  0.0 49.8 jit_solution(3213000198818827159)
XLA Ops:
  0.7 47.4 %gather_and_contract.1.src_ref = f32[128,6400]{1,0:T(8,128)S(1)} custom-call(f32[8,2,256]{2,1,0:T(2,128)} %amp_hbm.1, f32[2,8,6400]{2,1,0:T(8,128)} %int_hbm.1, s32[2,128]{1,0:T(2,128)} %bitcast.1, f32[200]{0:T(256)} %eocc_hbm.1, f32[800]{0:T(1024)} %evir_hbm.1, s32[1]{0:T(128)S(6)} %copy.7.off_ref), custom_call_target="tpu_custom_call" | custom-call | flops 2516582400 | bytes 3686400 | tf_op jit(solution)/shard_map/gather_and_contract/pallas_call | solution.py:434
  48.0 1.8 %store.1 = f32[128,6400]{1,0:T(8,128)} custom-call(f32[128,6400]{1,0:T(8,128)S(1)} %gather_and_contract.1.src_ref), custom_call_target="tpu_custom_call" | custom-call | bytes 3276800 | tf_op jit(solution)/shard_map/store/pallas_call | solution.py:476
